TPU v7x, 32 devices: a whole 2x2x4 slice. The times are simulated.
32 devices in a mesh: section: 2 (over x), dp: 16 (over z, y, core).
Axes of the slice: x: 2, y: 2, z: 4, core: 2. Of those that a mesh axis runs over, the one named last changes fastest.
Arguments:
- activations: bfloat16 [2, 2048, 5120], P('section', 'dp'), may hold values from -200 to 200, as said below
- upstream: bfloat16 [2, 2048, 5120], P('section', 'dp'), may hold values from -120 to 120, as said below
- section_norm_gain: float32 [2, 5120], P('section'), may hold values from 0.1 to 1.9
- adapter_down_weight: bfloat16 [2, 16, 5120], P('section'), may hold values from -0.078125 to 0.078125
- adapter_up_weight: bfloat16 [2, 16, 5120], P('section'), may hold values from -0.078125 to 0.078125
Outputs:
- passed: bfloat16 [2, 2048, 5120], P('section', 'dp')
- grad_pair: bfloat16 [2, 163840], P('section', 'dp')
Inputs may be any that keep to these rules, and one draw needn't show every extreme that they name: `activations`: activations of one token position share a part across replicas; rows and features have different scales. `upstream`: gradients of one token position share a part across replicas.
All inputs are finite; a program needn't handle non-finite values.
Results may differ from a plain program's by a relative error of at most 0.0034.
Values may be sent and summed in bfloat16 or wider, within the bound.
A program may use at most 64 MiB of HBM per device.

v0:
```python
import jax
import jax.numpy as jnp
from jax import lax
from jax.sharding import PartitionSpec as P

norm_eps = 1e-05
pair_eps = 1e-06
adapter_scale = 2.0


def swapped(value, axis, bit):
    mask = 2**bit
    pairs = [(source, source ^ mask) for source in range(lax.axis_size(axis))]
    return lax.ppermute(value, axis, pairs)


def from_behind(x, axis, by):
    size = lax.axis_size(axis)
    pairs = [(i, i + by) for i in range(size) if 0 <= i + by < size]
    return lax.ppermute(x, axis, pairs)


def replica_backward(inputs, incoming_gradient, gain_row, down_rows, upward_rows):
    widened = inputs.astype(jnp.float32)
    inverse = lax.rsqrt(jnp.mean(widened * widened, axis=-1, keepdims=True) + norm_eps)
    scaled = widened * inverse
    normed = (scaled * gain_row).astype(jnp.bfloat16)
    reduced_gradient = jnp.einsum(
        "sh,gh->sg", normed, down_rows, preferred_element_type=jnp.float32
    ).astype(jnp.bfloat16)
    count_of_rows = inputs.shape[0]
    upward_term = (
        adapter_scale
        * jnp.einsum(
            "tk,td->kd", reduced_gradient, incoming_gradient, preferred_element_type=jnp.float32
        )
        / count_of_rows
    )
    backward_lowrank = (
        adapter_scale
        * jnp.einsum(
            "sh,gh->sg", incoming_gradient, upward_rows, preferred_element_type=jnp.float32
        )
    ).astype(jnp.bfloat16)
    down_term = (
        jnp.einsum("tk,td->kd", backward_lowrank, normed, preferred_element_type=jnp.float32)
        / count_of_rows
    )
    back_norm = (
        jnp.einsum("tk,kd->td", backward_lowrank, down_rows, preferred_element_type=jnp.float32)
        * gain_row
    )
    centre = jnp.mean(back_norm * scaled, axis=-1, keepdims=True)
    passed = incoming_gradient.astype(jnp.float32) + inverse * (back_norm - scaled * centre)
    return (passed.astype(jnp.bfloat16), jnp.stack([down_term, upward_term]))


def doubling_tree(grad_pair):
    vector = grad_pair.reshape(2, -1)
    devices = lax.axis_size("dp")
    tree_levels = devices.bit_length() - 1
    for level_bit in range(tree_levels):
        partner = swapped(vector, "dp", level_bit)
        inner_sum = jnp.sum(vector * partner, axis=1, keepdims=True)
        own_square = jnp.sum(vector * vector, axis=1, keepdims=True)
        far_square = jnp.sum(partner * partner, axis=1, keepdims=True)
        keep_coef = 1.0 - inner_sum / (2.0 * (own_square + pair_eps))
        take_coef = 1.0 - inner_sum / (2.0 * (far_square + pair_eps))
        vector = keep_coef * vector + take_coef * partner
    flat_vector = vector.reshape(-1)
    slice_width = flat_vector.shape[0] // devices
    own_slice = lax.dynamic_slice_in_dim(
        flat_vector, lax.axis_index("dp") * slice_width, slice_width, 0
    )
    return own_slice.astype(jnp.bfloat16)[None]


def per_device(activations, upstream, section_norm_gain, adapter_down_weight, adapter_up_weight):
    passed_local, grad_pair = replica_backward(
        activations[0],
        upstream[0],
        section_norm_gain[0],
        adapter_down_weight[0],
        adapter_up_weight[0],
    )
    shifted = from_behind(passed_local[None], "section", -1)
    merged_gradient = doubling_tree(grad_pair)
    return (shifted, merged_gradient)


def solution(mesh):
    return jax.shard_map(
        per_device,
        mesh=mesh,
        in_specs=(
            P("section", "dp", None),
            P("section", "dp", None),
            P("section", None),
            P("section", None, None),
            P("section", None, None),
        ),
        out_specs=(P("section", "dp", None), P("section", "dp")),
        check_vma=False,
    )
```

profile of v0, /device:TPU:0, one launch (start us, length us, event | category | flops | bytes accessed | tf_op | source)
XLA Modules:
  0.0 82.7 jit_solution(16367113642206507500)
XLA Ops:
  0.7 1.8 %fusion.13 = f32[128]{0:T(128)S(1)} fusion(bf16[1,128,5120]{2,1,0:T(8,128)(2,1)} %param.5), kind=kLoop, calls=%fused_computation.18 | loop fusion | flops 1965952 | bytes 1311232 | tf_op jit(solution)/shard_map/reduce_sum | solution.py:25
  2.5 1.8 %fusion.34 = bf16[128,16]{0,1:T(8,128)(2,1)S(1)} fusion(bf16[1,128,5120]{2,1,0:T(8,128)(2,1)} %param.6, bf16[1,16,5120]{2,1,0:T(8,128)(2,1)} %param.9), kind=kOutput, calls=%fused_computation.33 | convolution fusion | flops 20975616 | bytes 1478656 | tf_op jit(solution)/shard_map/sh,gh->sg/dot_general | solution.py:41
  4.3 1.2 %fusion = f32[1,1,16,5120]{3,2,1,0:T(8,128)S(1)} fusion(bf16[1,128,5120]{2,1,0:T(8,128)(2,1)S(1)} %copy-done.2, bf16[1,128,5120]{2,1,0:T(8,128)(2,1)S(1)} %copy-done.1, f32[5120]{0:T(1024)S(1)} %bitcast.80, f32[128]{0:T(128)S(1)} %add_rsqrt_fusion, bf16[1,16,5120]{2,1,0:T(8,128)(2,1)S(1)} %copy-done), kind=kOutput, calls=%fused_computation.2 | convolution fusion | flops 44648448 | bytes 3133952 | tf_op jit(solution)/shard_map/tk,td->kd/dot_general | solution.py:34
  5.9 0.5 fusion.1
  6.7 0.6 pad_maximum_fusion
  7.3 0.5 collective-permute-start.1
  7.8 1.7 %collective-permute-done.1 = f32[2,81920]{1,0:T(2,128)S(1)} collective-permute-done((f32[2,81920]{1,0:T(2,128)S(1)}, f32[2,81920]{1,0:T(2,128)S(1)}, u32[]{:S(2)}, u32[]{:S(2)}) %collective-permute-start.1) | collective-permute-done | bytes 655392 | tf_op jit(solution)/shard_map/ppermute | solution.py:14
  9.5 1.5 %multiply_reduce_fusion.10 = (f32[2]{0:T(128)S(1)}, f32[2]{0:T(128)S(1)}, f32[2]{0:T(128)S(1)}) fusion(f32[2,81920]{1,0:T(2,128)S(1)} %collective-permute-done.1, f32[1,81920]{1,0:T(1,128)S(1)} %bitcast.74, f32[1,81920]{1,0:T(1,128)S(1)} %bitcast.77), kind=kLoop, calls=%fused_computation.49 | loop fusion | flops 1146874 | bytes 1310744 | tf_op jit(solution)/shard_map/reduce_sum | solution.py:65
  11.0 0.7 multiply_add_fusion.2
  11.8 2.9 %collective-permute-start.2 = (f32[2,81920]{1,0:T(2,128)S(1)}, f32[2,81920]{1,0:T(2,128)S(1)}, u32[]{:S(2)}, u32[]{:S(2)}) collective-permute-start(f32[2,81920]{1,0:T(2,128)S(1)} %multiply_add_fusion.2), channel_id=1, source_target_pairs={{0,2},{1,3},{2,0},{3,1},{4,6},{5,7},{6,4},{7,5},{8,10},{9,11},{10,... | collective-permute-start | bytes 1966088 | tf_op jit(solution)/shard_map/ppermute | solution.py:14
  14.7 0.7 fusion.7
  15.4 14.4 %collective-permute-done.2 = f32[2,81920]{1,0:T(2,128)S(1)} collective-permute-done((f32[2,81920]{1,0:T(2,128)S(1)}, f32[2,81920]{1,0:T(2,128)S(1)}, u32[]{:S(2)}, u32[]{:S(2)}) %collective-permute-start.2) | collective-permute-done | bytes 655392 | tf_op jit(solution)/shard_map/ppermute | solution.py:14
  29.8 1.1 %multiply_reduce_fusion.7 = (f32[2]{0:T(128)S(1)}, f32[2]{0:T(128)S(1)}, f32[2]{0:T(128)S(1)}) fusion(f32[2,81920]{1,0:T(2,128)S(1)} %multiply_add_fusion.2, f32[2,81920]{1,0:T(2,128)S(1)} %collective-permute-done.2), kind=kLoop, calls=%fused_computation.45 | loop fusion | flops 983034 | bytes 1310744 | tf_op jit(solution)/shard_map/reduce_sum | solution.py:65
  31.2 1.9 %collective-permute-start.3 = (f32[2,81920]{1,0:T(2,128)S(1)}, f32[2,81920]{1,0:T(2,128)S(1)}, u32[]{:S(2)}, u32[]{:S(2)}) collective-permute-start(f32[2,81920]{1,0:T(2,128)S(1)} %multiply_add_fusion.1), channel_id=1, source_target_pairs={{0,4},{1,5},{2,6},{3,7},{4,0},{5,1},{6,2},{7,3},{8,12},{9,13},{10,... | collective-permute-start | bytes 1966088 | tf_op jit(solution)/shard_map/ppermute | solution.py:14
  33.1 1.9 %fusion.20 = bf16[1,128,5120]{2,1,0:T(8,128)(2,1)} fusion(f32[128,5120]{1,0:T(8,128)S(1)} %get-tuple-element.23, bf16[1,128,5120]{2,1,0:T(8,128)(2,1)S(1)} %copy-done.1, bf16[1,128,5120]{2,1,0:T(8,128)(2,1)S(1)} %copy-done.2, f32[128]{0:T(128)S(1)} %broadcast_multiply_fusion, f32[128]{0:T(128)S(1)} %add_rsqrt_fusion), kind=kLoop, calls=%fused_computation.23 | loop fusion | flops 5242880 | bytes 6554624 | tf_op jit(solution)/shard_map/broadcast_in_dim | solution.py:86
  35.0 1.3 %collective-permute-start = (bf16[1,128,5120]{2,1,0:T(8,128)(2,1)}, bf16[1,128,5120]{2,1,0:T(8,128)(2,1)S(1)}, u32[]{:S(2)}, u32[]{:S(2)}) collective-permute-start(bf16[1,128,5120]{2,1,0:T(8,128)(2,1)} %fusion.20), channel_id=1, source_target_pairs={{16,0},{17,1},{18,2},{19,3},{20,4},{21,5},{22,6},{23,7},{24,8},{25... | collective-permute-start | bytes 3932168 | tf_op jit(solution)/shard_map/ppermute | solution.py:20
  36.3 11.3 %collective-permute-done.3 = f32[2,81920]{1,0:T(2,128)S(1)} collective-permute-done((f32[2,81920]{1,0:T(2,128)S(1)}, f32[2,81920]{1,0:T(2,128)S(1)}, u32[]{:S(2)}, u32[]{:S(2)}) %collective-permute-start.3) | collective-permute-done | bytes 655392 | tf_op jit(solution)/shard_map/ppermute | solution.py:14
  47.6 1.1 %multiply_reduce_fusion.4 = (f32[2]{0:T(128)S(1)}, f32[2]{0:T(128)S(1)}, f32[2]{0:T(128)S(1)}) fusion(f32[2,81920]{1,0:T(2,128)S(1)} %multiply_add_fusion.1, f32[2,81920]{1,0:T(2,128)S(1)} %collective-permute-done.3), kind=kLoop, calls=%fused_computation.41 | loop fusion | flops 983034 | bytes 1310744 | tf_op jit(solution)/shard_map/reduce_sum | solution.py:65
  49.0 2.6 %collective-permute-start.4 = (f32[2,81920]{1,0:T(2,128)S(1)}, f32[2,81920]{1,0:T(2,128)S(1)}, u32[]{:S(2)}, u32[]{:S(2)}) collective-permute-start(f32[2,81920]{1,0:T(2,128)S(1)} %multiply_add_fusion), channel_id=1, source_target_pairs={{0,8},{1,9},{2,10},{3,11},{4,12},{5,13},{6,14},{7,15},{8,0},{9,1},... | collective-permute-start | bytes 1966088 | tf_op jit(solution)/shard_map/ppermute | solution.py:14
  51.6 15.2 %collective-permute-done = bf16[1,128,5120]{2,1,0:T(8,128)(2,1)S(1)} collective-permute-done((bf16[1,128,5120]{2,1,0:T(8,128)(2,1)}, bf16[1,128,5120]{2,1,0:T(8,128)(2,1)S(1)}, u32[]{:S(2)}, u32[]{:S(2)}) %collective-permute-start) | collective-permute-done | bytes 1310752 | tf_op jit(solution)/shard_map/ppermute | solution.py:20
  66.8 12.6 %collective-permute-done.4 = f32[2,81920]{1,0:T(2,128)S(1)} collective-permute-done((f32[2,81920]{1,0:T(2,128)S(1)}, f32[2,81920]{1,0:T(2,128)S(1)}, u32[]{:S(2)}, u32[]{:S(2)}) %collective-permute-start.4) | collective-permute-done | bytes 655392 | tf_op jit(solution)/shard_map/ppermute | solution.py:14
  79.4 1.1 %multiply_reduce_fusion.1 = (f32[2]{0:T(128)S(1)}, f32[2]{0:T(128)S(1)}, f32[2]{0:T(128)S(1)}) fusion(f32[2,81920]{1,0:T(2,128)S(1)} %multiply_add_fusion, f32[2,81920]{1,0:T(2,128)S(1)} %collective-permute-done.4), kind=kLoop, calls=%fused_computation.37 | loop fusion | flops 983034 | bytes 1310744 | tf_op jit(solution)/shard_map/reduce_sum | solution.py:65
  81.0 0.6 broadcast_in_dim.5
  81.6 1.1 %copy.11 = bf16[1,128,5120]{2,1,0:T(8,128)(2,1)} copy(bf16[1,128,5120]{2,1,0:T(8,128)(2,1)S(1)} %collective-permute-done) | data formatting | bytes 2621440
  (21 shorter events, 2.1 us)
Async XLA Ops:
  0.6 3.6 %copy-start = (bf16[1,16,5120]{2,1,0:T(8,128)(2,1)S(1)}, bf16[1,16,5120]{2,1,0:T(8,128)(2,1)}, u32[]{:S(2)}) copy-start(bf16[1,16,5120]{2,1,0:T(8,128)(2,1)} %param.8) | copy-start | bytes 491524
  0.6 3.6 %copy-start.1 = (bf16[1,128,5120]{2,1,0:T(8,128)(2,1)S(1)}, bf16[1,128,5120]{2,1,0:T(8,128)(2,1)}, u32[]{:S(2)}) copy-start(bf16[1,128,5120]{2,1,0:T(8,128)(2,1)} %param.5) | copy-start | bytes 3932164
  0.7 3.6 %copy-start.2 = (bf16[1,128,5120]{2,1,0:T(8,128)(2,1)S(1)}, bf16[1,128,5120]{2,1,0:T(8,128)(2,1)}, u32[]{:S(2)}) copy-start(bf16[1,128,5120]{2,1,0:T(8,128)(2,1)} %param.6) | copy-start | bytes 3932164
  0.7 3.6 %copy-start.3 = (f32[1,5120]{1,0:T(1,128)S(1)}, f32[1,5120]{1,0:T(1,128)}, u32[]{:S(2)}) copy-start(f32[1,5120]{1,0:T(1,128)} %param.7) | copy-start | bytes 61444
  7.3 2.3 %collective-permute-start.1 = (f32[2,81920]{1,0:T(2,128)S(1)}, f32[2,81920]{1,0:T(2,128)S(1)}, u32[]{:S(2)}, u32[]{:S(2)}) collective-permute-start(f32[2,81920]{1,0:T(2,128)S(1)} %pad_maximum_fusion), channel_id=1, source_target_pairs={{0,1},{1,0},{2,3},{3,2},{4,5},{5,4},{6,7},{7,6},{8,9},{9,8},{10,11... | collective-permute-start | bytes 1966088 | tf_op jit(solution)/shard_map/ppermute | solution.py:14
  11.8 18.0 %collective-permute-start.2 = (f32[2,81920]{1,0:T(2,128)S(1)}, f32[2,81920]{1,0:T(2,128)S(1)}, u32[]{:S(2)}, u32[]{:S(2)}) collective-permute-start(f32[2,81920]{1,0:T(2,128)S(1)} %multiply_add_fusion.2), channel_id=1, source_target_pairs={{0,2},{1,3},{2,0},{3,1},{4,6},{5,7},{6,4},{7,5},{8,10},{9,11},{10,... | collective-permute-start | bytes 1966088 | tf_op jit(solution)/shard_map/ppermute | solution.py:14
  31.2 16.3 %collective-permute-start.3 = (f32[2,81920]{1,0:T(2,128)S(1)}, f32[2,81920]{1,0:T(2,128)S(1)}, u32[]{:S(2)}, u32[]{:S(2)}) collective-permute-start(f32[2,81920]{1,0:T(2,128)S(1)} %multiply_add_fusion.1), channel_id=1, source_target_pairs={{0,4},{1,5},{2,6},{3,7},{4,0},{5,1},{6,2},{7,3},{8,12},{9,13},{10,... | collective-permute-start | bytes 1966088 | tf_op jit(solution)/shard_map/ppermute | solution.py:14
  35.0 31.8 %collective-permute-start = (bf16[1,128,5120]{2,1,0:T(8,128)(2,1)}, bf16[1,128,5120]{2,1,0:T(8,128)(2,1)S(1)}, u32[]{:S(2)}, u32[]{:S(2)}) collective-permute-start(bf16[1,128,5120]{2,1,0:T(8,128)(2,1)} %fusion.20), channel_id=1, source_target_pairs={{16,0},{17,1},{18,2},{19,3},{20,4},{21,5},{22,6},{23,7},{24,8},{25... | collective-permute-start | bytes 3932168 | tf_op jit(solution)/shard_map/ppermute | solution.py:20
  49.0 30.4 %collective-permute-start.4 = (f32[2,81920]{1,0:T(2,128)S(1)}, f32[2,81920]{1,0:T(2,128)S(1)}, u32[]{:S(2)}, u32[]{:S(2)}) collective-permute-start(f32[2,81920]{1,0:T(2,128)S(1)} %multiply_add_fusion), channel_id=1, source_target_pairs={{0,8},{1,9},{2,10},{3,11},{4,12},{5,13},{6,14},{7,15},{8,0},{9,1},... | collective-permute-start | bytes 1966088 | tf_op jit(solution)/shard_map/ppermute | solution.py:14
where the time goes:
time: 82.9 us; the launch traced here: 82.7 us
  waiting for transfers between devices  55.2 us (67%)
  other arithmetic  10.9 us (13%)
  starting transfers between devices  9.17 us (11%)
  matrix products  4.12 us (5%)
  local copies, waits for them, and re-layouts  2.47 us (3%)
    ppermute x4, waiting for transfers between devices, swapped(): return lax.ppermute(value, axis, pairs)  40 us
    ppermute x1, waiting for transfers between devices, from_behind(): return lax.ppermute(x, axis, pairs)  15.2 us
    ppermute x4, starting transfers between devices, swapped(): return lax.ppermute(value, axis, pairs)  7.89 us
    reduce_sum x4, other arithmetic, doubling_tree(): own_square = jnp.sum(vector * vector, axis=1, keepdims=True)  4.65 us
    broadcast_in_dim x1, other arithmetic, per_device(): shifted = from_behind(passed_local[None], 'section', -1)  1.88 us
    unnamed x12, local copies, waits for them, and re-layouts  1.82 us
    reduce_sum x1, other arithmetic, replica_backward(): jnp.mean(widened * widened, axis=-1, keepdims=True) + norm_eps  1.8 us
    dot_general x1, matrix products, replica_backward(): jnp.einsum('sh,gh->sg', incoming_gradient, upward_rows, preferred_element...  1.76 us
  transfers between devices with their start and end apart: 5, of which 5 were waited for; matrix products, arithmetic and copies ran while one was open for 5% of the time, Pallas kernels for 0%

commit v1 on v0

v1 whole, which is shorter than its diff:
```python
import functools

import jax
import jax.numpy as jnp
from jax import lax
from jax.experimental import pallas as pl
from jax.experimental.pallas import tpu as pltpu
from jax.sharding import PartitionSpec as P

norm_eps = 1e-05
pair_eps = 1e-06
adapter_scale = 2.0
LANES = 128
MESH = pl.DeviceIdType.MESH
F32 = jnp.float32
BF16 = jnp.bfloat16

BLOCK_ROWS = (32, 32, 32, 32)
EARLY_BLOCKS = 2
CHUNK = 1024


def contract_last(a, b):
    return lax.dot_general(a, b, (((1,), (1,)), ((), ())), preferred_element_type=F32)


def contract_first(a, b):
    return lax.dot_general(a, b, (((0,), (0,)), ((), ())), preferred_element_type=F32)


def tree_coefficients(gram, n):
    row = lax.broadcasted_iota(jnp.int32, (n, LANES), 0)
    lane = lax.broadcasted_iota(jnp.int32, (n, LANES), 1)
    same = row == lane
    coef = jnp.ones((n, 1), F32)
    step = 1
    while step < n:
        own = jnp.where(same, gram, 0.0)
        cross = jnp.where(lane == (row ^ step), gram, 0.0)

        def factor(axis):
            own_square = jnp.maximum(jnp.sum(own, axis=axis, keepdims=True), 0.0)
            inner = jnp.sum(cross, axis=axis, keepdims=True)
            return 1.0 - inner / (2.0 * (own_square + pair_eps))

        down, across = factor(1), factor(0)
        coef = coef * down
        gram = gram * down * across
        gram = gram + jnp.where(
            (row & step) != 0, pltpu.roll(gram, step, 0), pltpu.roll(gram, n - step, 0)
        )
        gram = gram + jnp.where(
            (lane & step) != 0, pltpu.roll(gram, step, 1), pltpu.roll(gram, LANES - step, 1)
        )
        step *= 2
    return coef


def kernel(
    sections, n, q, pad,
    x_hbm, g_hbm, gain_hbm, down_hbm, up_hbm,
    passed_ref, pair_ref,
    x_ref, g_ref, gain_ref, down_ref, up_ref, normed_ref, grad_ref, zero_ref,
    red_ref, low_ref, inv_ref, cen_ref,
    flat_ref, vsend, vrecv, vwide, gram_send, gram_recv, coef_ref,
    w_sem, x_sem, g_sem, zero_sem,
    pass_send, pass_recv, v_send_sem, v_recv_sem, gram_send_sem, gram_recv_sem,
):
    tokens, width = x_ref.shape
    rank = down_ref.shape[0]
    tiles = width // LANES
    half = n // 2
    section = lax.axis_index("section")
    me = lax.axis_index("dp")
    sends = section > 0
    receives = section < sections - 1
    before = lax.rem(section + sections - 1, sections)

    starts = [sum(BLOCK_ROWS[:b]) for b in range(len(BLOCK_ROWS))]
    blocks = [pl.ds(start, rows) for start, rows in zip(starts, BLOCK_ROWS)]

    weights = [
        pltpu.make_async_copy(up_hbm.at[0], up_ref, w_sem.at[0]),
        pltpu.make_async_copy(down_hbm.at[0], down_ref, w_sem.at[1]),
        pltpu.make_async_copy(gain_hbm, gain_ref, w_sem.at[2]),
    ]
    x_in = [pltpu.make_async_copy(x_hbm.at[0, r], x_ref.at[r], x_sem.at[b]) for b, r in enumerate(blocks)]
    g_in = [pltpu.make_async_copy(g_hbm.at[0, r], g_ref.at[r], g_sem.at[b]) for b, r in enumerate(blocks)]
    x_in[0].start()
    weights[0].start()
    g_in[0].start()
    weights[1].start()
    weights[2].start()
    for b in range(1, len(blocks)):
        x_in[b].start()
        g_in[b].start()

    barrier = pltpu.get_barrier_semaphore()

    def greet(k, carry):
        pl.semaphore_signal(
            barrier, inc=1, device_id=(section, lax.rem(me + k, n)), device_id_type=MESH
        )
        return carry

    @pl.when(sends)
    def _():
        pl.semaphore_signal(barrier, inc=1, device_id=(section - 1, me), device_id_type=MESH)

    @pl.when(receives)
    def _():
        pl.semaphore_signal(barrier, inc=1, device_id=(section + 1, me), device_id_type=MESH)

    lax.fori_loop(1, n, greet, 0)

    def pass_copy(b):
        return pltpu.make_async_remote_copy(
            src_ref=grad_ref.at[blocks[b]],
            dst_ref=passed_ref.at[0, blocks[b]],
            send_sem=pass_send.at[b],
            recv_sem=pass_recv.at[b],
            device_id=(before, me),
            device_id_type=MESH,
        )

    columns = [slice(c, c + CHUNK) for c in range(0, width, CHUNK)]

    def statistics(b):
        rows = slice(starts[b], starts[b] + BLOCK_ROWS[b])
        x_in[b].wait()
        squares = jnp.zeros((BLOCK_ROWS[b], LANES), F32)
        for c in range(0, width, LANES):
            wide = x_ref[rows, c : c + LANES].astype(F32)
            squares = squares + wide * wide
        inverse = lax.rsqrt(jnp.sum(squares, axis=1, keepdims=True) / width + norm_eps)
        g_in[b].wait()
        if b == 0:
            for copy in weights:
                copy.wait()
        low = jnp.zeros((BLOCK_ROWS[b], rank), F32)
        red = jnp.zeros((BLOCK_ROWS[b], rank), F32)
        for c in columns:
            low = low + contract_last(g_ref[rows, c], up_ref[:, c])
            normed = (x_ref[rows, c].astype(F32) * inverse * gain_ref[:, c]).astype(BF16)
            normed_ref[rows, c] = normed
            red = red + contract_last(normed, down_ref[:, c])
        low = (adapter_scale * low).astype(BF16)
        low_ref[rows, :] = low
        red_ref[rows, :] = red.astype(BF16)
        inv_ref[rows, :] = inverse
        cen_ref[rows, :] = jnp.sum(low.astype(F32) * red, axis=1, keepdims=True) / width

    def relay(b):
        rows = slice(starts[b], starts[b] + BLOCK_ROWS[b])

        @pl.when(sends)
        def _():
            inverse = inv_ref[rows, :]
            shift = inverse * cen_ref[rows, :]
            low = low_ref[rows, :]
            for c in columns:
                back = jnp.dot(low, down_ref[:, c], preferred_element_type=F32) * gain_ref[:, c]
                grad = g_ref[rows, c].astype(F32) + inverse * (back - x_ref[rows, c].astype(F32) * shift)
                grad_ref[rows, c] = grad.astype(BF16)
            pass_copy(b).start()

    statistics(0)
    from_sections = jnp.where(sends, 1, 0) + jnp.where(receives, 1, 0)
    pl.semaphore_wait(barrier, n - 1 + from_sections)
    relay(0)

    @pl.when(jnp.logical_not(receives))
    def _():
        zero_ref[...] = jnp.zeros_like(zero_ref)
        for b, r in enumerate(blocks):
            pltpu.make_async_copy(
                zero_ref.at[pl.ds(0, BLOCK_ROWS[b])], passed_ref.at[0, r], zero_sem.at[b]
            ).start()

    for b in range(1, len(blocks)):
        statistics(b)
        if b < EARLY_BLOCKS:
            relay(b)

    if pad != q:
        flat_ref[...] = jnp.zeros_like(flat_ref)
        stride = (tiles // q) * pad
    else:
        stride = tiles
    for c in range(0, width, CHUNK):
        down_term = contract_first(low_ref[...], normed_ref[:, c : c + CHUNK]) / tokens
        up_term = adapter_scale * contract_first(red_ref[...], g_ref[:, c : c + CHUNK]) / tokens
        for t, term in enumerate((down_term, up_term)):
            for inner in range(CHUNK // LANES):
                tile = c // LANES + inner
                place = tile if pad == q else (tile // q) * pad + tile % q
                flat_ref[pl.ds(t * half * pad + place, rank, stride=stride), :] = (
                    term[:, inner * LANES : (inner + 1) * LANES]
                )

    def pack(d, carry):
        vsend[d] = flat_ref[pl.ds(pl.multiple_of(d * pad, 8), pad), :].astype(BF16)
        return carry

    lax.fori_loop(0, n, pack, 0)

    def v_copy(k):
        to = lax.rem(me + k, n)
        return pltpu.make_async_remote_copy(
            src_ref=vsend.at[to],
            dst_ref=vrecv.at[me],
            send_sem=v_send_sem.at[k],
            recv_sem=v_recv_sem.at[k],
            device_id=(section, to),
            device_id_type=MESH,
        )

    def v_arrival(k):
        source = lax.rem(me + n - k, n)
        return pltpu.make_async_remote_copy(
            src_ref=vsend.at[source],
            dst_ref=vrecv.at[source],
            send_sem=v_send_sem.at[k],
            recv_sem=v_recv_sem.at[k],
            device_id=(section, source),
            device_id_type=MESH,
        )

    def v_start(k, carry):
        v_copy(k).start()
        return carry

    lax.fori_loop(1, n, v_start, 0)
    vwide[me] = vsend[me].astype(F32)

    for b in range(EARLY_BLOCKS, len(blocks)):
        relay(b)

    def v_wait(k, carry):
        v_arrival(k).wait_recv()
        source = lax.rem(me + n - k, n)
        vwide[source] = vrecv[source].astype(F32)
        return carry

    lax.fori_loop(1, n, v_wait, 0)

    lane = lax.broadcasted_iota(jnp.int32, (n, LANES), 1)

    def gram_column(i, gram):
        products = jnp.sum(vwide[...] * vwide[i][None], axis=1)
        return jnp.where(lane == i, jnp.sum(products, axis=1, keepdims=True), gram)

    gram_send[...] = lax.fori_loop(0, n, gram_column, jnp.zeros((n, LANES), F32))

    base = (me // half) * half
    place = me - base

    def gram_copy(k):
        to = lax.rem(place + k, half)
        return pltpu.make_async_remote_copy(
            src_ref=gram_send,
            dst_ref=gram_recv.at[place],
            send_sem=gram_send_sem.at[k],
            recv_sem=gram_recv_sem.at[k],
            device_id=(section, base + to),
            device_id_type=MESH,
        )

    def gram_arrival(k):
        source = lax.rem(place + half - k, half)
        return pltpu.make_async_remote_copy(
            src_ref=gram_send,
            dst_ref=gram_recv.at[source],
            send_sem=gram_send_sem.at[k],
            recv_sem=gram_recv_sem.at[k],
            device_id=(section, base + source),
            device_id_type=MESH,
        )

    def gram_start(k, carry):
        gram_copy(k).start()
        return carry

    lax.fori_loop(1, half, gram_start, 0)
    gram_recv[place] = gram_send[...]

    def gram_wait(k, carry):
        gram_arrival(k).wait_recv()
        return carry

    lax.fori_loop(1, half, gram_wait, 0)

    coef = tree_coefficients(jnp.sum(gram_recv[...], axis=0), n)
    coef_ref[...] = jnp.broadcast_to(coef, (n, LANES))

    def weigh(i, total):
        return total + coef_ref[pl.ds(i, 1), :] * vwide[i]

    total = lax.fori_loop(0, n, weigh, jnp.zeros((pad, LANES), F32))
    for tile in range(q):
        pair_ref[:, tile * LANES : (tile + 1) * LANES] = total[tile : tile + 1, :].astype(BF16)

    def sent(k, carry):
        v_copy(k).wait_send()
        return carry

    lax.fori_loop(1, n, sent, 0)

    def gram_sent(k, carry):
        gram_copy(k).wait_send()
        return carry

    lax.fori_loop(1, half, gram_sent, 0)

    @pl.when(jnp.logical_not(receives))
    def _():
        for b, r in enumerate(blocks):
            pltpu.make_async_copy(
                zero_ref.at[pl.ds(0, BLOCK_ROWS[b])], passed_ref.at[0, r], zero_sem.at[b]
            ).wait()

    @pl.when(sends)
    def _():
        for b in range(len(blocks)):
            pass_copy(b).wait_send()

    @pl.when(receives)
    def _():
        for b in range(len(blocks)):
            pass_copy(b).wait_recv()


def per_device(sections, n, activations, upstream, gain, down, up):
    _, tokens, width = activations.shape
    rank = down.shape[1]
    share = 2 * rank * width // n
    q = share // LANES
    pad = q if share >= width else -(-q // 16) * 16
    count = len(BLOCK_ROWS)
    anywhere = pl.BlockSpec(memory_space=pl.ANY)
    return pl.pallas_call(
        functools.partial(kernel, sections, n, q, pad),
        out_shape=(
            jax.ShapeDtypeStruct(activations.shape, BF16),
            jax.ShapeDtypeStruct((1, share), BF16),
        ),
        in_specs=[pl.BlockSpec(memory_space=pltpu.HBM)] * 5,
        out_specs=(anywhere, pl.BlockSpec(memory_space=pltpu.VMEM)),
        scratch_shapes=[
            pltpu.VMEM((tokens, width), BF16),
            pltpu.VMEM((tokens, width), BF16),
            pltpu.VMEM((1, width), F32),
            pltpu.VMEM((rank, width), BF16),
            pltpu.VMEM((rank, width), BF16),
            pltpu.VMEM((tokens, width), BF16),
            pltpu.VMEM((tokens, width), BF16),
            pltpu.VMEM((max(BLOCK_ROWS), width), BF16),
            pltpu.VMEM((tokens, rank), BF16),
            pltpu.VMEM((tokens, rank), BF16),
            pltpu.VMEM((tokens, 1), F32),
            pltpu.VMEM((tokens, 1), F32),
            pltpu.VMEM((n * pad, LANES), F32),
            pltpu.VMEM((n, pad, LANES), BF16),
            pltpu.VMEM((n, pad, LANES), BF16),
            pltpu.VMEM((n, pad, LANES), F32),
            pltpu.VMEM((n, LANES), F32),
            pltpu.VMEM((n // 2, n, LANES), F32),
            pltpu.VMEM((n, LANES), F32),
            pltpu.SemaphoreType.DMA((3,)),
            pltpu.SemaphoreType.DMA((count,)),
            pltpu.SemaphoreType.DMA((count,)),
            pltpu.SemaphoreType.DMA((count,)),
            pltpu.SemaphoreType.DMA((count,)),
            pltpu.SemaphoreType.DMA((count,)),
            pltpu.SemaphoreType.DMA((n,)),
            pltpu.SemaphoreType.DMA((n,)),
            pltpu.SemaphoreType.DMA((n,)),
            pltpu.SemaphoreType.DMA((n,)),
        ],
        compiler_params=pltpu.CompilerParams(
            collective_id=0, has_side_effects=True, vmem_limit_bytes=40 * 2**20
        ),
        cost_estimate=pl.CostEstimate(
            flops=12 * tokens * width * rank, bytes_accessed=6 * tokens * width, transcendentals=0
        ),
    )(activations, upstream, gain, down, up)


def solution(mesh):
    return jax.shard_map(
        functools.partial(per_device, mesh.shape["section"], mesh.shape["dp"]),
        mesh=mesh,
        in_specs=(
            P("section", "dp", None),
            P("section", "dp", None),
            P("section", None),
            P("section", None, None),
            P("section", None, None),
        ),
        out_specs=(P("section", "dp", None), P("section", "dp")),
        check_vma=False,
    )
```

time: 82.9 us -> 46.7 us (0.56)
  waiting for transfers between devices: 55.2 us -> 0 us
  Pallas kernels: 0 us -> 38.9 us
  other arithmetic: 10.9 us -> 0 us
  starting transfers between devices: 9.17 us -> 0 us
  local copies, waits for them, and re-layouts: 2.47 us -> 6.86 us
  matrix products: 4.12 us -> 0 us
    ppermute x5 -> x0, waiting for transfers between devices: 55.2 us -> none  [the longest x4 40 us: swapped(): return lax.ppermute(value, axis, pairs)]
    pallas_call x0 -> x1, Pallas kernels: none -> 38.9 us  [per_device(): pl.pallas_call(functools.partial(kernel, sections, n, q, pad), out_shape=...]
    ppermute x5 -> x0, starting transfers between devices: 9.17 us -> none  [the longest x4 7.89 us: swapped(): return lax.ppermute(value, axis, pairs)]
    reduce_sum x5 -> x0, other arithmetic: 6.45 us -> none  [the longest x4 4.65 us: doubling_tree(): own_square = jnp.sum(vector * vector, axis=1, keepdims=True)]
    unnamed x12, local copies, waits for them, and re-layouts: 1.82 us -> 6.86 us
    dot_general x4 -> x0, matrix products: 4.12 us -> none  [the longest x1 1.76 us: replica_backward(): jnp.einsum('sh,gh->sg', incoming_gradient, upward_rows, preferred_element...]
    broadcast_in_dim x1 -> x0, other arithmetic: 1.88 us -> none  [per_device(): shifted = from_behind(passed_local[None], 'section', -1)]
    add x3 -> x0, other arithmetic: 1.55 us -> none  [doubling_tree(): vector = keep_coef * vector + take_coef * partner]
  transfers between devices with their start and end apart: 5 -> 0, of which waited for: 5 -> 0; matrix products, arithmetic and copies ran while one was open for 5% -> 0% of each run, Pallas kernels for 0% -> 0%
where the time goes in v1:
time: 46.7 us; the launch traced here: 46.4 us
  Pallas kernels  38.9 us (83%)
  local copies, waits for them, and re-layouts  6.86 us (15%)
  between operations  0.65 us (1%)
    pallas_call x1, Pallas kernels, per_device(): pl.pallas_call(functools.partial(kernel, sections, n, q, pad), out_shape=...  38.9 us
    unnamed x12, local copies, waits for them, and re-layouts  6.86 us

profile of v1, /device:TPU:0, one launch (start us, length us, event | category | flops | bytes accessed | tf_op | source)
XLA Modules:
  0.0 46.4 jit_solution(5209318077537181846)
XLA Ops:
  0.6 0.0 copy-start
  0.6 1.3 %copy-done = bf16[1,128,5120]{2,1,0:T(8,128)(2,1)S(1)} copy-done((bf16[1,128,5120]{2,1,0:T(8,128)(2,1)S(1)}, bf16[1,128,5120]{2,1,0:T(8,128)(2,1)}, u32[]{:S(2)}) %copy-start) | copy-done | bytes 1310744
  1.9 0.0 copy-start.1
  2.0 1.3 %copy-done.1 = bf16[1,128,5120]{2,1,0:T(8,128)(2,1)S(1)} copy-done((bf16[1,128,5120]{2,1,0:T(8,128)(2,1)S(1)}, bf16[1,128,5120]{2,1,0:T(8,128)(2,1)}, u32[]{:S(2)}) %copy-start.1) | copy-done | bytes 1310744
  3.3 0.0 copy-start.2
  3.3 0.9 %copy-done.2 = bf16[1,16,5120]{2,1,0:T(8,128)(2,1)S(1)} copy-done((bf16[1,16,5120]{2,1,0:T(8,128)(2,1)S(1)}, bf16[1,16,5120]{2,1,0:T(8,128)(2,1)}, u32[]{:S(2)}) %copy-start.2) | copy-done | bytes 163864
  4.2 0.0 copy-start.3
  4.2 0.9 %copy-done.3 = bf16[1,16,5120]{2,1,0:T(8,128)(2,1)S(1)} copy-done((bf16[1,16,5120]{2,1,0:T(8,128)(2,1)S(1)}, bf16[1,16,5120]{2,1,0:T(8,128)(2,1)}, u32[]{:S(2)}) %copy-start.3) | copy-done | bytes 163864
  5.1 0.0 copy-start.4
  5.1 0.7 %copy-done.4 = f32[1,5120]{1,0:T(1,128)S(1)} copy-done((f32[1,5120]{1,0:T(1,128)S(1)}, f32[1,5120]{1,0:T(1,128)}, u32[]{:S(2)}) %copy-start.4) | copy-done | bytes 20504
  5.8 38.9 %shard_map.68 = (bf16[1,128,5120]{2,1,0:T(8,128)(2,1)S(1)}, bf16[1,10240]{1,0:T(2,128)(2,1)S(1)}) custom-call(bf16[1,128,5120]{2,1,0:T(8,128)(2,1)S(1)} %copy-done, bf16[1,128,5120]{2,1,0:T(8,128)(2,1)S(1)} %copy-done.1, f32[1,5120]{1,0:T(1,128)S(1)} %copy-done.4, bf16[1,16,5120]{2,1,0:T(8,128)(2,1)S(1)} %copy-done.2, bf16[1,16,5120]{2,1,0:T(8,128)(2,1)S(1)} %copy-done.3), custom_call_target="tpu_custom_call" | custom-call | flops 125829120 | bytes 3932160 | tf_op jit(solution)/shard_map/pallas_call | solution.py:341
  44.7 1.1 %copy.9 = bf16[1,128,5120]{2,1,0:T(8,128)(2,1)} copy(bf16[1,128,5120]{2,1,0:T(8,128)(2,1)S(1)} %get-tuple-element.4) | data formatting | bytes 2621440
  45.8 0.6 %copy.10 = bf16[1,10240]{1,0:T(2,128)(2,1)} copy(bf16[1,10240]{1,0:T(2,128)(2,1)S(1)} %get-tuple-element.5) | data formatting | bytes 40960
Async XLA Ops:
  0.6 1.3 %copy-start = (bf16[1,128,5120]{2,1,0:T(8,128)(2,1)S(1)}, bf16[1,128,5120]{2,1,0:T(8,128)(2,1)}, u32[]{:S(2)}) copy-start(bf16[1,128,5120]{2,1,0:T(8,128)(2,1)} %x_hbm.1) | copy-start | bytes 3932164
  1.9 1.3 %copy-start.1 = (bf16[1,128,5120]{2,1,0:T(8,128)(2,1)S(1)}, bf16[1,128,5120]{2,1,0:T(8,128)(2,1)}, u32[]{:S(2)}) copy-start(bf16[1,128,5120]{2,1,0:T(8,128)(2,1)} %g_hbm.1) | copy-start | bytes 3932164
  3.3 0.9 %copy-start.2 = (bf16[1,16,5120]{2,1,0:T(8,128)(2,1)S(1)}, bf16[1,16,5120]{2,1,0:T(8,128)(2,1)}, u32[]{:S(2)}) copy-start(bf16[1,16,5120]{2,1,0:T(8,128)(2,1)} %down_hbm.1) | copy-start | bytes 491524
  4.2 0.9 %copy-start.3 = (bf16[1,16,5120]{2,1,0:T(8,128)(2,1)S(1)}, bf16[1,16,5120]{2,1,0:T(8,128)(2,1)}, u32[]{:S(2)}) copy-start(bf16[1,16,5120]{2,1,0:T(8,128)(2,1)} %up_hbm.1) | copy-start | bytes 491524
  5.1 0.7 %copy-start.4 = (f32[1,5120]{1,0:T(1,128)S(1)}, f32[1,5120]{1,0:T(1,128)}, u32[]{:S(2)}) copy-start(f32[1,5120]{1,0:T(1,128)} %gain_hbm.1) | copy-start | bytes 61444

commit v2 on v1

--- a/solution.py
+++ b/solution.py
@@ -15,8 +15,8 @@
 F32 = jnp.float32
 BF16 = jnp.bfloat16
 
-BLOCK_ROWS = (32, 32, 32, 32)
-EARLY_BLOCKS = 2
+BLOCK_ROWS = (16, 16, 32, 64)
+EARLY_BLOCKS = 3
 CHUNK = 1024
 
 
@@ -383,7 +383,7 @@
         cost_estimate=pl.CostEstimate(
             flops=12 * tokens * width * rank, bytes_accessed=6 * tokens * width, transcendentals=0
         ),
-    )(activations, upstream, gain, down, up)
+    )(*[pltpu.with_memory_space_constraint(a, pltpu.HBM) for a in (activations, upstream, gain, down, up)])
 
 
 def solution(mesh):

time: 46.7 us -> 40.1 us (0.86)
  local copies, waits for them, and re-layouts: 6.86 us -> 1.68 us
  Pallas kernels: 38.9 us -> 37.6 us
    unnamed x12 -> x2, local copies, waits for them, and re-layouts: 6.86 us -> 1.68 us
    pallas_call x1, Pallas kernels: 38.9 us -> 37.6 us  [per_device(): pl.pallas_call(functools.partial(kernel, sections, n, q, pad), out_shape=...]
where the time goes in v2:
time: 40.1 us; the launch traced here: 39.9 us
  Pallas kernels  37.6 us (94%)
  local copies, waits for them, and re-layouts  1.68 us (4%)
  between operations  0.64 us (2%)
    pallas_call x1, Pallas kernels, per_device(): pl.pallas_call(functools.partial(kernel, sections, n, q, pad), out_shape=...  37.6 us
    unnamed x2, local copies, waits for them, and re-layouts  1.68 us

profile of v2, /device:TPU:0, one launch (start us, length us, event | category | flops | bytes accessed | tf_op | source)
XLA Modules:
  0.0 39.9 jit_solution(15381245957204167307)
XLA Ops:
  0.6 37.6 %shard_map.68 = (bf16[1,128,5120]{2,1,0:T(8,128)(2,1)S(1)}, bf16[1,10240]{1,0:T(2,128)(2,1)S(1)}) custom-call(bf16[1,128,5120]{2,1,0:T(8,128)(2,1)} %x_hbm.1, bf16[1,128,5120]{2,1,0:T(8,128)(2,1)} %g_hbm.1, f32[1,5120]{1,0:T(1,128)} %gain_hbm.1, bf16[1,16,5120]{2,1,0:T(8,128)(2,1)} %down_hbm.1, bf16[1,16,5120]{2,1,0:T(8,128)(2,1)} %up_hbm.1), custom_call_target="tpu_custom_call" | custom-call | flops 125829120 | bytes 3932160 | tf_op jit(solution)/shard_map/pallas_call | solution.py:341
  38.3 1.1 %copy.9 = bf16[1,128,5120]{2,1,0:T(8,128)(2,1)} copy(bf16[1,128,5120]{2,1,0:T(8,128)(2,1)S(1)} %get-tuple-element.4) | data formatting | bytes 2621440
  39.3 0.6 %copy.10 = bf16[1,10240]{1,0:T(2,128)(2,1)} copy(bf16[1,10240]{1,0:T(2,128)(2,1)S(1)} %get-tuple-element.5) | data formatting | bytes 40960

commit v3 on v2

--- a/solution.py
+++ b/solution.py
@@ -16,7 +16,7 @@
 BF16 = jnp.bfloat16
 
 BLOCK_ROWS = (16, 16, 32, 64)
-EARLY_BLOCKS = 3
+PIECES = 8
 CHUNK = 1024
 
 
@@ -179,8 +179,7 @@
 
     for b in range(1, len(blocks)):
         statistics(b)
-        if b < EARLY_BLOCKS:
-            relay(b)
+        relay(b)
 
     if pad != q:
         flat_ref[...] = jnp.zeros_like(flat_ref)
@@ -233,9 +232,6 @@
     lax.fori_loop(1, n, v_start, 0)
     vwide[me] = vsend[me].astype(F32)
 
-    for b in range(EARLY_BLOCKS, len(blocks)):
-        relay(b)
-
     def v_wait(k, carry):
         v_arrival(k).wait_recv()
         source = lax.rem(me + n - k, n)
@@ -330,6 +326,18 @@
             pass_copy(b).wait_recv()
 
 
+def store_results(passed_in, pair_in, passed_out, pair_out, sem):
+    rows = passed_in.shape[1] // PIECES
+    copies = [pltpu.make_async_copy(pair_in, pair_out, sem.at[PIECES])]
+    for i in range(PIECES):
+        piece = pl.ds(i * rows, rows)
+        copies.append(pltpu.make_async_copy(passed_in.at[0, piece], passed_out.at[0, piece], sem.at[i]))
+    for copy in copies:
+        copy.start()
+    for copy in copies:
+        copy.wait()
+
+
 def per_device(sections, n, activations, upstream, gain, down, up):
     _, tokens, width = activations.shape
     rank = down.shape[1]
@@ -338,12 +346,13 @@
     pad = q if share >= width else -(-q // 16) * 16
     count = len(BLOCK_ROWS)
     anywhere = pl.BlockSpec(memory_space=pl.ANY)
-    return pl.pallas_call(
+    shapes = (
+        jax.ShapeDtypeStruct(activations.shape, BF16),
+        jax.ShapeDtypeStruct((1, share), BF16),
+    )
+    held = pl.pallas_call(
         functools.partial(kernel, sections, n, q, pad),
-        out_shape=(
-            jax.ShapeDtypeStruct(activations.shape, BF16),
-            jax.ShapeDtypeStruct((1, share), BF16),
-        ),
+        out_shape=shapes,
         in_specs=[pl.BlockSpec(memory_space=pltpu.HBM)] * 5,
         out_specs=(anywhere, pl.BlockSpec(memory_space=pltpu.VMEM)),
         scratch_shapes=[
@@ -384,6 +393,13 @@
             flops=12 * tokens * width * rank, bytes_accessed=6 * tokens * width, transcendentals=0
         ),
     )(*[pltpu.with_memory_space_constraint(a, pltpu.HBM) for a in (activations, upstream, gain, down, up)])
+    return pl.pallas_call(
+        store_results,
+        out_shape=shapes,
+        in_specs=[anywhere, anywhere],
+        out_specs=(anywhere, anywhere),
+        scratch_shapes=[pltpu.SemaphoreType.DMA((PIECES + 1,))],
+    )(*held)
 
 
 def solution(mesh):

time: 40.1 us -> 82.2 us (2.05)
  Pallas kernels: 37.6 us -> 79.8 us
    pallas_call x0 -> x1, Pallas kernels: none -> 42.1 us  [per_device(): pl.pallas_call(store_results, out_shape=shapes, in_specs=[anywhere, anywh...]
    unnamed x2 -> x4, local copies, waits for them, and re-layouts: 1.68 us -> 1.67 us
where the time goes in v3:
time: 82.2 us; the launch traced here: 82.1 us
  Pallas kernels  79.8 us (97%)
  local copies, waits for them, and re-layouts  1.67 us (2%)
    pallas_call x1, Pallas kernels, per_device(): pl.pallas_call(store_results, out_shape=shapes, in_specs=[anywhere, anywh...  42.1 us
    pallas_call x1, Pallas kernels, per_device(): pl.pallas_call(functools.partial(kernel, sections, n, q, pad), out_shape=...  37.6 us
    unnamed x4, local copies, waits for them, and re-layouts  1.67 us

profile of v3, /device:TPU:0, one launch (start us, length us, event | category | flops | bytes accessed | tf_op | source)
XLA Modules:
  0.0 82.1 jit_solution(9269802976433847888)
XLA Ops:
  0.6 37.6 %shard_map.68 = (bf16[1,128,5120]{2,1,0:T(8,128)(2,1)S(1)}, bf16[1,10240]{1,0:T(2,128)(2,1)S(1)}) custom-call(bf16[1,128,5120]{2,1,0:T(8,128)(2,1)} %x_hbm.1, bf16[1,128,5120]{2,1,0:T(8,128)(2,1)} %g_hbm.1, f32[1,5120]{1,0:T(1,128)} %gain_hbm.1, bf16[1,16,5120]{2,1,0:T(8,128)(2,1)} %down_hbm.1, bf16[1,16,5120]{2,1,0:T(8,128)(2,1)} %up_hbm.1), custom_call_target="tpu_custom_call" | custom-call | flops 125829120 | bytes 3932160 | tf_op jit(solution)/shard_map/pallas_call | solution.py:353
  38.3 0.0 copy-start
  38.3 1.1 %copy-done = bf16[1,128,5120]{2,1,0:T(8,128)(2,1)} copy-done((bf16[1,128,5120]{2,1,0:T(8,128)(2,1)}, bf16[1,128,5120]{2,1,0:T(8,128)(2,1)S(1)}, u32[]{:S(2)}) %copy-start) | copy-done | bytes 1310744
  39.3 0.0 copy-start.1
  39.3 0.6 copy-done.1
  39.9 42.1 %shard_map.69 = (bf16[1,128,5120]{2,1,0:T(8,128)(2,1)}, bf16[1,10240]{1,0:T(2,128)(2,1)}) custom-call(bf16[1,128,5120]{2,1,0:T(8,128)(2,1)} %copy-done, bf16[1,10240]{1,0:T(2,128)(2,1)} %copy-done.1), custom_call_target="tpu_custom_call" | custom-call | tf_op jit(solution)/shard_map/pallas_call | solution.py:396
Async XLA Ops:
  38.3 1.1 %copy-start = (bf16[1,128,5120]{2,1,0:T(8,128)(2,1)}, bf16[1,128,5120]{2,1,0:T(8,128)(2,1)S(1)}, u32[]{:S(2)}) copy-start(bf16[1,128,5120]{2,1,0:T(8,128)(2,1)S(1)} %get-tuple-element.4.passed_in) | copy-start | bytes 3932164
  39.3 0.6 copy-start.1

commit v4 on v3

--- a/solution.py
+++ b/solution.py
@@ -61,10 +61,11 @@
     x_hbm, g_hbm, gain_hbm, down_hbm, up_hbm,
     passed_ref, pair_ref,
     x_ref, g_ref, gain_ref, down_ref, up_ref, normed_ref, grad_ref, zero_ref,
-    red_ref, low_ref, inv_ref, cen_ref,
+    red_ref, low_ref,
     flat_ref, vsend, vrecv, vwide, gram_send, gram_recv, coef_ref,
     w_sem, x_sem, g_sem, zero_sem,
     pass_send, pass_recv, v_send_sem, v_recv_sem, gram_send_sem, gram_recv_sem,
+    here_sem, round_sem, ready_sem,
 ):
     tokens, width = x_ref.shape
     rank = down_ref.shape[0]
@@ -97,21 +98,22 @@
 
     barrier = pltpu.get_barrier_semaphore()
 
-    def greet(k, carry):
-        pl.semaphore_signal(
-            barrier, inc=1, device_id=(section, lax.rem(me + k, n)), device_id_type=MESH
-        )
-        return carry
-
-    @pl.when(sends)
-    def _():
-        pl.semaphore_signal(barrier, inc=1, device_id=(section - 1, me), device_id_type=MESH)
+    def to_peers(semaphore):
+        def signal(k, carry):
+            pl.semaphore_signal(
+                semaphore, inc=1, device_id=(section, lax.rem(me + k, n)), device_id_type=MESH
+            )
+            return carry
+
+        lax.fori_loop(1, n, signal, 0)
 
     @pl.when(receives)
     def _():
         pl.semaphore_signal(barrier, inc=1, device_id=(section + 1, me), device_id_type=MESH)
 
-    lax.fori_loop(1, n, greet, 0)
+    @pl.when(section == 0)
+    def _():
+        to_peers(barrier)
 
     def pass_copy(b):
         return pltpu.make_async_remote_copy(
@@ -123,51 +125,46 @@
             device_id_type=MESH,
         )
 
-    columns = [slice(c, c + CHUNK) for c in range(0, width, CHUNK)]
-
-    def statistics(b):
-        rows = slice(starts[b], starts[b] + BLOCK_ROWS[b])
+    def work(b):
+        count = BLOCK_ROWS[b]
+        rows = slice(starts[b], starts[b] + count)
+        chunk = CHUNK if count <= 32 else CHUNK // 2
+        columns = [slice(c, c + chunk) for c in range(0, width, chunk)]
         x_in[b].wait()
-        squares = jnp.zeros((BLOCK_ROWS[b], LANES), F32)
+        g_in[b].wait()
+        if b == 0:
+            for copy in weights:
+                copy.wait()
+        low = jnp.zeros((count, rank), F32)
+        for c in columns:
+            low = low + contract_last(g_ref[rows, c], up_ref[:, c])
+        low = (adapter_scale * low).astype(BF16)
+        squares = jnp.zeros((count, LANES), F32)
         for c in range(0, width, LANES):
             wide = x_ref[rows, c : c + LANES].astype(F32)
             squares = squares + wide * wide
         inverse = lax.rsqrt(jnp.sum(squares, axis=1, keepdims=True) / width + norm_eps)
-        g_in[b].wait()
-        if b == 0:
-            for copy in weights:
-                copy.wait()
-        low = jnp.zeros((BLOCK_ROWS[b], rank), F32)
-        red = jnp.zeros((BLOCK_ROWS[b], rank), F32)
+        red = jnp.zeros((count, rank), F32)
         for c in columns:
-            low = low + contract_last(g_ref[rows, c], up_ref[:, c])
             normed = (x_ref[rows, c].astype(F32) * inverse * gain_ref[:, c]).astype(BF16)
             normed_ref[rows, c] = normed
             red = red + contract_last(normed, down_ref[:, c])
-        low = (adapter_scale * low).astype(BF16)
         low_ref[rows, :] = low
         red_ref[rows, :] = red.astype(BF16)
-        inv_ref[rows, :] = inverse
-        cen_ref[rows, :] = jnp.sum(low.astype(F32) * red, axis=1, keepdims=True) / width
-
-    def relay(b):
-        rows = slice(starts[b], starts[b] + BLOCK_ROWS[b])
+        shift = inverse * (jnp.sum(low.astype(F32) * red, axis=1, keepdims=True) / width)
+        for c in columns:
+            back = jnp.dot(low, down_ref[:, c], preferred_element_type=F32) * gain_ref[:, c]
+            grad = g_ref[rows, c].astype(F32) + inverse * (back - x_ref[rows, c].astype(F32) * shift)
+            grad_ref[rows, c] = grad.astype(BF16)
 
         @pl.when(sends)
         def _():
-            inverse = inv_ref[rows, :]
-            shift = inverse * cen_ref[rows, :]
-            low = low_ref[rows, :]
-            for c in columns:
-                back = jnp.dot(low, down_ref[:, c], preferred_element_type=F32) * gain_ref[:, c]
-                grad = g_ref[rows, c].astype(F32) + inverse * (back - x_ref[rows, c].astype(F32) * shift)
-                grad_ref[rows, c] = grad.astype(BF16)
+            if b == 0:
+                pl.semaphore_wait(barrier, 1)
+                pl.semaphore_signal(here_sem, inc=1, device_id=(before, me), device_id_type=MESH)
             pass_copy(b).start()
 
-    statistics(0)
-    from_sections = jnp.where(sends, 1, 0) + jnp.where(receives, 1, 0)
-    pl.semaphore_wait(barrier, n - 1 + from_sections)
-    relay(0)
+    work(0)
 
     @pl.when(jnp.logical_not(receives))
     def _():
@@ -178,8 +175,16 @@
             ).start()
 
     for b in range(1, len(blocks)):
-        statistics(b)
-        relay(b)
+        work(b)
+
+    @pl.when(section == 0)
+    def _():
+        pl.semaphore_wait(barrier, n - 1)
+
+        @pl.when(receives)
+        def _():
+            pl.semaphore_wait(here_sem, 1)
+            to_peers(round_sem)
 
     if pad != q:
         flat_ref[...] = jnp.zeros_like(flat_ref)
@@ -202,6 +207,20 @@
         return carry
 
     lax.fori_loop(0, n, pack, 0)
+
+    @pl.when(sends)
+    def _():
+        pl.semaphore_wait(ready_sem, 1)
+
+        @pl.when(receives)
+        def _():
+            pl.semaphore_wait(here_sem, 1)
+            to_peers(round_sem)
+
+    @pl.when(receives)
+    def _():
+        pl.semaphore_wait(round_sem, n - 1)
+        pl.semaphore_signal(ready_sem, inc=1, device_id=(section + 1, me), device_id_type=MESH)
 
     def v_copy(k):
         to = lax.rem(me + k, n)
@@ -366,8 +385,6 @@
             pltpu.VMEM((max(BLOCK_ROWS), width), BF16),
             pltpu.VMEM((tokens, rank), BF16),
             pltpu.VMEM((tokens, rank), BF16),
-            pltpu.VMEM((tokens, 1), F32),
-            pltpu.VMEM((tokens, 1), F32),
             pltpu.VMEM((n * pad, LANES), F32),
             pltpu.VMEM((n, pad, LANES), BF16),
             pltpu.VMEM((n, pad, LANES), BF16),
@@ -385,6 +402,9 @@
             pltpu.SemaphoreType.DMA((n,)),
             pltpu.SemaphoreType.DMA((n,)),
             pltpu.SemaphoreType.DMA((n,)),
+            pltpu.SemaphoreType.REGULAR,
+            pltpu.SemaphoreType.REGULAR,
+            pltpu.SemaphoreType.REGULAR,
         ],
         compiler_params=pltpu.CompilerParams(
             collective_id=0, has_side_effects=True, vmem_limit_bytes=40 * 2**20
@@ -396,7 +416,7 @@
     return pl.pallas_call(
         store_results,
         out_shape=shapes,
-        in_specs=[anywhere, anywhere],
+        in_specs=[pl.BlockSpec(memory_space=pltpu.VMEM)] * 2,
         out_specs=(anywhere, anywhere),
         scratch_shapes=[pltpu.SemaphoreType.DMA((PIECES + 1,))],
     )(*held)

time: 82.2 us -> 39.4 us (0.48)
  Pallas kernels: 79.8 us -> 36.9 us
    pallas_call x1, Pallas kernels: 42.1 us -> 2.45 us  [per_device(): pl.pallas_call(store_results, out_shape=shapes, in_specs=[pl.BlockSpec(me...]
    pallas_call x1, Pallas kernels: 37.6 us -> 34.4 us  [per_device(): pl.pallas_call(functools.partial(kernel, sections, n, q, pad), out_shape=...]
where the time goes in v4:
time: 39.4 us; the launch traced here: 39.2 us
  Pallas kernels  36.9 us (94%)
  local copies, waits for them, and re-layouts  1.67 us (4%)
  between operations  0.65 us (2%)
    pallas_call x1, Pallas kernels, per_device(): pl.pallas_call(functools.partial(kernel, sections, n, q, pad), out_shape=...  34.4 us
    pallas_call x1, Pallas kernels, per_device(): pl.pallas_call(store_results, out_shape=shapes, in_specs=[pl.BlockSpec(me...  2.45 us
    unnamed x4, local copies, waits for them, and re-layouts  1.67 us

profile of v4, /device:TPU:0, one launch (start us, length us, event | category | flops | bytes accessed | tf_op | source)
XLA Modules:
  0.0 39.2 jit_solution(11163412846713113874)
XLA Ops:
  0.6 34.4 %shard_map.68 = (bf16[1,128,5120]{2,1,0:T(8,128)(2,1)S(1)}, bf16[1,10240]{1,0:T(2,128)(2,1)S(1)}) custom-call(bf16[1,128,5120]{2,1,0:T(8,128)(2,1)} %x_hbm.1, bf16[1,128,5120]{2,1,0:T(8,128)(2,1)} %g_hbm.1, f32[1,5120]{1,0:T(1,128)} %gain_hbm.1, bf16[1,16,5120]{2,1,0:T(8,128)(2,1)} %down_hbm.1, bf16[1,16,5120]{2,1,0:T(8,128)(2,1)} %up_hbm.1), custom_call_target="tpu_custom_call" | custom-call | flops 125829120 | bytes 3932160 | tf_op jit(solution)/shard_map/pallas_call | solution.py:372
  35.1 0.0 copy-start
  35.1 1.1 %copy-done = bf16[1,128,5120]{2,1,0:T(8,128)(2,1)} copy-done((bf16[1,128,5120]{2,1,0:T(8,128)(2,1)}, bf16[1,128,5120]{2,1,0:T(8,128)(2,1)S(1)}, u32[]{:S(2)}) %copy-start) | copy-done | bytes 1310744
  36.1 0.0 copy-start.1
  36.1 0.6 %copy-done.1 = bf16[1,10240]{1,0:T(2,128)(2,1)} copy-done((bf16[1,10240]{1,0:T(2,128)(2,1)}, bf16[1,10240]{1,0:T(2,128)(2,1)S(1)}, u32[]{:S(2)}) %copy-start.1) | copy-done | bytes 20504
  36.7 2.5 %shard_map.69 = (bf16[1,128,5120]{2,1,0:T(8,128)(2,1)}, bf16[1,10240]{1,0:T(2,128)(2,1)}) custom-call(bf16[1,128,5120]{2,1,0:T(8,128)(2,1)} %copy-done, bf16[1,10240]{1,0:T(2,128)(2,1)} %copy-done.1), custom_call_target="tpu_custom_call" | custom-call | tf_op jit(solution)/shard_map/pallas_call | solution.py:416
Async XLA Ops:
  35.1 1.1 %copy-start = (bf16[1,128,5120]{2,1,0:T(8,128)(2,1)}, bf16[1,128,5120]{2,1,0:T(8,128)(2,1)S(1)}, u32[]{:S(2)}) copy-start(bf16[1,128,5120]{2,1,0:T(8,128)(2,1)S(1)} %get-tuple-element.4.passed_in) | copy-start | bytes 3932164
  36.1 0.6 %copy-start.1 = (bf16[1,10240]{1,0:T(2,128)(2,1)}, bf16[1,10240]{1,0:T(2,128)(2,1)S(1)}, u32[]{:S(2)}) copy-start(bf16[1,10240]{1,0:T(2,128)(2,1)S(1)} %get-tuple-element.5.pair_in) | copy-start | bytes 61444

commit v5 on v4

--- a/solution.py
+++ b/solution.py
@@ -16,7 +16,6 @@
 BF16 = jnp.bfloat16
 
 BLOCK_ROWS = (16, 16, 32, 64)
-PIECES = 8
 CHUNK = 1024
 
 
@@ -88,13 +87,9 @@
     x_in = [pltpu.make_async_copy(x_hbm.at[0, r], x_ref.at[r], x_sem.at[b]) for b, r in enumerate(blocks)]
     g_in = [pltpu.make_async_copy(g_hbm.at[0, r], g_ref.at[r], g_sem.at[b]) for b, r in enumerate(blocks)]
     x_in[0].start()
-    weights[0].start()
     g_in[0].start()
-    weights[1].start()
-    weights[2].start()
-    for b in range(1, len(blocks)):
-        x_in[b].start()
-        g_in[b].start()
+    for copy in weights:
+        copy.start()
 
     barrier = pltpu.get_barrier_semaphore()
 
@@ -135,6 +130,9 @@
         if b == 0:
             for copy in weights:
                 copy.wait()
+            for later in range(1, len(blocks)):
+                x_in[later].start()
+                g_in[later].start()
         low = jnp.zeros((count, rank), F32)
         for c in columns:
             low = low + contract_last(g_ref[rows, c], up_ref[:, c])
@@ -345,18 +343,6 @@
             pass_copy(b).wait_recv()
 
 
-def store_results(passed_in, pair_in, passed_out, pair_out, sem):
-    rows = passed_in.shape[1] // PIECES
-    copies = [pltpu.make_async_copy(pair_in, pair_out, sem.at[PIECES])]
-    for i in range(PIECES):
-        piece = pl.ds(i * rows, rows)
-        copies.append(pltpu.make_async_copy(passed_in.at[0, piece], passed_out.at[0, piece], sem.at[i]))
-    for copy in copies:
-        copy.start()
-    for copy in copies:
-        copy.wait()
-
-
 def per_device(sections, n, activations, upstream, gain, down, up):
     _, tokens, width = activations.shape
     rank = down.shape[1]
@@ -369,7 +355,7 @@
         jax.ShapeDtypeStruct(activations.shape, BF16),
         jax.ShapeDtypeStruct((1, share), BF16),
     )
-    held = pl.pallas_call(
+    return pl.pallas_call(
         functools.partial(kernel, sections, n, q, pad),
         out_shape=shapes,
         in_specs=[pl.BlockSpec(memory_space=pltpu.HBM)] * 5,
@@ -413,13 +399,6 @@
             flops=12 * tokens * width * rank, bytes_accessed=6 * tokens * width, transcendentals=0
         ),
     )(*[pltpu.with_memory_space_constraint(a, pltpu.HBM) for a in (activations, upstream, gain, down, up)])
-    return pl.pallas_call(
-        store_results,
-        out_shape=shapes,
-        in_specs=[pl.BlockSpec(memory_space=pltpu.VMEM)] * 2,
-        out_specs=(anywhere, anywhere),
-        scratch_shapes=[pltpu.SemaphoreType.DMA((PIECES + 1,))],
-    )(*held)
 
 
 def solution(mesh):

time: 39.4 us -> 36.7 us (0.931)
  Pallas kernels: 36.9 us -> 34.2 us
    pallas_call x1 -> x0, Pallas kernels: 2.45 us -> none  [per_device(): pl.pallas_call(store_results, out_shape=shapes, in_specs=[pl.BlockSpec(me...]
    unnamed x4 -> x2, local copies, waits for them, and re-layouts: 1.67 us -> 1.68 us
where the time goes in v5:
time: 36.7 us; the launch traced here: 36.5 us
  Pallas kernels  34.2 us (93%)
  local copies, waits for them, and re-layouts  1.68 us (5%)
  between operations  0.64 us (2%)
    pallas_call x1, Pallas kernels, per_device(): pl.pallas_call(functools.partial(kernel, sections, n, q, pad), out_shape=...  34.2 us
    unnamed x2, local copies, waits for them, and re-layouts  1.68 us

profile of v5, /device:TPU:0, one launch (start us, length us, event | category | flops | bytes accessed | tf_op | source)
XLA Modules:
  0.0 36.5 jit_solution(15354022426541296706)
XLA Ops:
  0.6 34.2 %shard_map.68 = (bf16[1,128,5120]{2,1,0:T(8,128)(2,1)S(1)}, bf16[1,10240]{1,0:T(2,128)(2,1)S(1)}) custom-call(bf16[1,128,5120]{2,1,0:T(8,128)(2,1)} %x_hbm.1, bf16[1,128,5120]{2,1,0:T(8,128)(2,1)} %g_hbm.1, f32[1,5120]{1,0:T(1,128)} %gain_hbm.1, bf16[1,16,5120]{2,1,0:T(8,128)(2,1)} %down_hbm.1, bf16[1,16,5120]{2,1,0:T(8,128)(2,1)} %up_hbm.1), custom_call_target="tpu_custom_call" | custom-call | flops 125829120 | bytes 3932160 | tf_op jit(solution)/shard_map/pallas_call | solution.py:358
  34.9 1.1 %copy.9 = bf16[1,128,5120]{2,1,0:T(8,128)(2,1)} copy(bf16[1,128,5120]{2,1,0:T(8,128)(2,1)S(1)} %get-tuple-element.4) | data formatting | bytes 2621440
  35.9 0.6 %copy.10 = bf16[1,10240]{1,0:T(2,128)(2,1)} copy(bf16[1,10240]{1,0:T(2,128)(2,1)S(1)} %get-tuple-element.5) | data formatting | bytes 40960

commit v6 on v4

--- a/solution.py
+++ b/solution.py
@@ -16,8 +16,8 @@
 BF16 = jnp.bfloat16
 
 BLOCK_ROWS = (16, 16, 32, 64)
+CHUNK = 1024
 PIECES = 8
-CHUNK = 1024
 
 
 def contract_last(a, b):
@@ -88,13 +88,9 @@
     x_in = [pltpu.make_async_copy(x_hbm.at[0, r], x_ref.at[r], x_sem.at[b]) for b, r in enumerate(blocks)]
     g_in = [pltpu.make_async_copy(g_hbm.at[0, r], g_ref.at[r], g_sem.at[b]) for b, r in enumerate(blocks)]
     x_in[0].start()
-    weights[0].start()
     g_in[0].start()
-    weights[1].start()
-    weights[2].start()
-    for b in range(1, len(blocks)):
-        x_in[b].start()
-        g_in[b].start()
+    for copy in weights:
+        copy.start()
 
     barrier = pltpu.get_barrier_semaphore()
 
@@ -135,6 +131,9 @@
         if b == 0:
             for copy in weights:
                 copy.wait()
+            for later in range(1, len(blocks)):
+                x_in[later].start()
+                g_in[later].start()
         low = jnp.zeros((count, rank), F32)
         for c in columns:
             low = low + contract_last(g_ref[rows, c], up_ref[:, c])
@@ -416,10 +415,10 @@
     return pl.pallas_call(
         store_results,
         out_shape=shapes,
-        in_specs=[pl.BlockSpec(memory_space=pltpu.VMEM)] * 2,
+        in_specs=[anywhere, anywhere],
         out_specs=(anywhere, anywhere),
         scratch_shapes=[pltpu.SemaphoreType.DMA((PIECES + 1,))],
-    )(*held)
+    )(*[pltpu.with_memory_space_constraint(value, pltpu.VMEM) for value in held])
 
 
 def solution(mesh):

time: 39.4 us -> 36.2 us (0.919)
  local copies, waits for them, and re-layouts: 1.67 us -> 0 us
  Pallas kernels: 36.9 us -> 35.4 us
    unnamed x4 -> x0, local copies, waits for them, and re-layouts: 1.67 us -> none
    pallas_call x1, Pallas kernels: 2.45 us -> 1.14 us  [per_device(): pl.pallas_call(store_results, out_shape=shapes, in_specs=[anywhere, anywh...]
where the time goes in v6:
time: 36.2 us; the launch traced here: 36 us
  Pallas kernels  35.4 us (98%)
  between operations  0.64 us (2%)
    pallas_call x1, Pallas kernels, per_device(): pl.pallas_call(functools.partial(kernel, sections, n, q, pad), out_shape=...  34.2 us
    pallas_call x1, Pallas kernels, per_device(): pl.pallas_call(store_results, out_shape=shapes, in_specs=[anywhere, anywh...  1.14 us

profile of v6, /device:TPU:0, one launch (start us, length us, event | category | flops | bytes accessed | tf_op | source)
XLA Modules:
  0.0 36.0 jit_solution(6460376389240525344)
XLA Ops:
  0.6 34.2 %shard_map.68 = (bf16[1,128,5120]{2,1,0:T(8,128)(2,1)S(1)}, bf16[1,10240]{1,0:T(2,128)(2,1)S(1)}) custom-call(bf16[1,128,5120]{2,1,0:T(8,128)(2,1)} %x_hbm.1, bf16[1,128,5120]{2,1,0:T(8,128)(2,1)} %g_hbm.1, f32[1,5120]{1,0:T(1,128)} %gain_hbm.1, bf16[1,16,5120]{2,1,0:T(8,128)(2,1)} %down_hbm.1, bf16[1,16,5120]{2,1,0:T(8,128)(2,1)} %up_hbm.1), custom_call_target="tpu_custom_call" | custom-call | flops 125829120 | bytes 3932160 | tf_op jit(solution)/shard_map/pallas_call | solution.py:371
  34.9 1.1 %shard_map.69 = (bf16[1,128,5120]{2,1,0:T(8,128)(2,1)}, bf16[1,10240]{1,0:T(2,128)(2,1)}) custom-call(bf16[1,128,5120]{2,1,0:T(8,128)(2,1)S(1)} %get-tuple-element.4.passed_in, bf16[1,10240]{1,0:T(2,128)(2,1)S(1)} %get-tuple-element.5.pair_in), custom_call_target="tpu_custom_call" | custom-call | tf_op jit(solution)/shard_map/pallas_call | solution.py:415

commit v7 on v6

--- a/solution.py
+++ b/solution.py
@@ -18,6 +18,7 @@
 BLOCK_ROWS = (16, 16, 32, 64)
 CHUNK = 1024
 PIECES = 8
+SEND_ROWS = 16
 
 
 def contract_last(a, b):
@@ -111,12 +112,13 @@
     def _():
         to_peers(barrier)
 
-    def pass_copy(b):
+    def pass_copy(i):
+        rows = pl.ds(i * SEND_ROWS, SEND_ROWS)
         return pltpu.make_async_remote_copy(
-            src_ref=grad_ref.at[blocks[b]],
-            dst_ref=passed_ref.at[0, blocks[b]],
-            send_sem=pass_send.at[b],
-            recv_sem=pass_recv.at[b],
+            src_ref=grad_ref.at[rows],
+            dst_ref=passed_ref.at[0, rows],
+            send_sem=pass_send.at[i],
+            recv_sem=pass_recv.at[i],
             device_id=(before, me),
             device_id_type=MESH,
         )
@@ -161,7 +163,8 @@
             if b == 0:
                 pl.semaphore_wait(barrier, 1)
                 pl.semaphore_signal(here_sem, inc=1, device_id=(before, me), device_id_type=MESH)
-            pass_copy(b).start()
+            for i in range(starts[b] // SEND_ROWS, (starts[b] + count) // SEND_ROWS):
+                pass_copy(i).start()
 
     work(0)
 
@@ -335,13 +338,13 @@
 
     @pl.when(sends)
     def _():
-        for b in range(len(blocks)):
-            pass_copy(b).wait_send()
+        for i in range(tokens // SEND_ROWS):
+            pass_copy(i).wait_send()
 
     @pl.when(receives)
     def _():
-        for b in range(len(blocks)):
-            pass_copy(b).wait_recv()
+        for i in range(tokens // SEND_ROWS):
+            pass_copy(i).wait_recv()
 
 
 def store_results(passed_in, pair_in, passed_out, pair_out, sem):
@@ -395,8 +398,8 @@
             pltpu.SemaphoreType.DMA((count,)),
             pltpu.SemaphoreType.DMA((count,)),
             pltpu.SemaphoreType.DMA((count,)),
-            pltpu.SemaphoreType.DMA((count,)),
-            pltpu.SemaphoreType.DMA((count,)),
+            pltpu.SemaphoreType.DMA((tokens // SEND_ROWS,)),
+            pltpu.SemaphoreType.DMA((tokens // SEND_ROWS,)),
             pltpu.SemaphoreType.DMA((n,)),
             pltpu.SemaphoreType.DMA((n,)),
             pltpu.SemaphoreType.DMA((n,)),

time: 36.2 us -> 36.2 us (level)
  no operation moved by 1% of the time
where the time goes in v7:
time: 36.2 us; the launch traced here: 36.1 us
  Pallas kernels  35.4 us (98%)
  between operations  0.64 us (2%)
    pallas_call x1, Pallas kernels, per_device(): pl.pallas_call(functools.partial(kernel, sections, n, q, pad), out_shape=...  34.3 us
    pallas_call x1, Pallas kernels, per_device(): pl.pallas_call(store_results, out_shape=shapes, in_specs=[anywhere, anywh...  1.14 us

profile of v7, /device:TPU:0, one launch (start us, length us, event | category | flops | bytes accessed | tf_op | source)
XLA Modules:
  0.0 36.1 jit_solution(15143527960114965501)
XLA Ops:
  0.6 34.3 %shard_map.68 = (bf16[1,128,5120]{2,1,0:T(8,128)(2,1)S(1)}, bf16[1,10240]{1,0:T(2,128)(2,1)S(1)}) custom-call(bf16[1,128,5120]{2,1,0:T(8,128)(2,1)} %x_hbm.1, bf16[1,128,5120]{2,1,0:T(8,128)(2,1)} %g_hbm.1, f32[1,5120]{1,0:T(1,128)} %gain_hbm.1, bf16[1,16,5120]{2,1,0:T(8,128)(2,1)} %down_hbm.1, bf16[1,16,5120]{2,1,0:T(8,128)(2,1)} %up_hbm.1), custom_call_target="tpu_custom_call" | custom-call | flops 125829120 | bytes 3932160 | tf_op jit(solution)/shard_map/pallas_call | solution.py:374
  34.9 1.1 %shard_map.69 = (bf16[1,128,5120]{2,1,0:T(8,128)(2,1)}, bf16[1,10240]{1,0:T(2,128)(2,1)}) custom-call(bf16[1,128,5120]{2,1,0:T(8,128)(2,1)S(1)} %get-tuple-element.4.passed_in, bf16[1,10240]{1,0:T(2,128)(2,1)S(1)} %get-tuple-element.5.pair_in), custom_call_target="tpu_custom_call" | custom-call | tf_op jit(solution)/shard_map/pallas_call | solution.py:418

commit v8 on v6

--- a/solution.py
+++ b/solution.py
@@ -17,7 +17,7 @@
 
 BLOCK_ROWS = (16, 16, 32, 64)
 CHUNK = 1024
-PIECES = 8
+PIECES = 4
 
 
 def contract_last(a, b):
@@ -126,6 +126,7 @@
         rows = slice(starts[b], starts[b] + count)
         chunk = CHUNK if count <= 32 else CHUNK // 2
         columns = [slice(c, c + chunk) for c in range(0, width, chunk)]
+        spans = columns if count > 16 else [slice(0, width)]
         x_in[b].wait()
         g_in[b].wait()
         if b == 0:
@@ -135,7 +136,7 @@
                 x_in[later].start()
                 g_in[later].start()
         low = jnp.zeros((count, rank), F32)
-        for c in columns:
+        for c in spans:
             low = low + contract_last(g_ref[rows, c], up_ref[:, c])
         low = (adapter_scale * low).astype(BF16)
         squares = jnp.zeros((count, LANES), F32)
@@ -144,7 +145,7 @@
             squares = squares + wide * wide
         inverse = lax.rsqrt(jnp.sum(squares, axis=1, keepdims=True) / width + norm_eps)
         red = jnp.zeros((count, rank), F32)
-        for c in columns:
+        for c in spans:
             normed = (x_ref[rows, c].astype(F32) * inverse * gain_ref[:, c]).astype(BF16)
             normed_ref[rows, c] = normed
             red = red + contract_last(normed, down_ref[:, c])
@@ -160,8 +161,9 @@
         def _():
             if b == 0:
                 pl.semaphore_wait(barrier, 1)
+            pass_copy(b).start()
+            if b == 0:
                 pl.semaphore_signal(here_sem, inc=1, device_id=(before, me), device_id_type=MESH)
-            pass_copy(b).start()
 
     work(0)
 

time: 36.2 us -> 36.1 us (level)
  no operation moved by 1% of the time
where the time goes in v8:
time: 36.1 us; the launch traced here: 36 us
  Pallas kernels  35.3 us (98%)
  between operations  0.64 us (2%)
    pallas_call x1, Pallas kernels, per_device(): pl.pallas_call(functools.partial(kernel, sections, n, q, pad), out_shape=...  34.2 us
    pallas_call x1, Pallas kernels, per_device(): pl.pallas_call(store_results, out_shape=shapes, in_specs=[anywhere, anywh...  1.11 us

profile of v8, /device:TPU:0, one launch (start us, length us, event | category | flops | bytes accessed | tf_op | source)
XLA Modules:
  0.0 36.0 jit_solution(8028020600305914151)
XLA Ops:
  0.6 34.2 %shard_map.68 = (bf16[1,128,5120]{2,1,0:T(8,128)(2,1)S(1)}, bf16[1,10240]{1,0:T(2,128)(2,1)S(1)}) custom-call(bf16[1,128,5120]{2,1,0:T(8,128)(2,1)} %x_hbm.1, bf16[1,128,5120]{2,1,0:T(8,128)(2,1)} %g_hbm.1, f32[1,5120]{1,0:T(1,128)} %gain_hbm.1, bf16[1,16,5120]{2,1,0:T(8,128)(2,1)} %down_hbm.1, bf16[1,16,5120]{2,1,0:T(8,128)(2,1)} %up_hbm.1), custom_call_target="tpu_custom_call" | custom-call | flops 125829120 | bytes 3932160 | tf_op jit(solution)/shard_map/pallas_call | solution.py:373
  34.9 1.1 %shard_map.69 = (bf16[1,128,5120]{2,1,0:T(8,128)(2,1)}, bf16[1,10240]{1,0:T(2,128)(2,1)}) custom-call(bf16[1,128,5120]{2,1,0:T(8,128)(2,1)S(1)} %get-tuple-element.4.passed_in, bf16[1,10240]{1,0:T(2,128)(2,1)S(1)} %get-tuple-element.5.pair_in), custom_call_target="tpu_custom_call" | custom-call | tf_op jit(solution)/shard_map/pallas_call | solution.py:417

commit v9 on v8

--- a/solution.py
+++ b/solution.py
@@ -15,7 +15,7 @@
 F32 = jnp.float32
 BF16 = jnp.bfloat16
 
-BLOCK_ROWS = (16, 16, 32, 64)
+BLOCK_ROWS = (16, 48, 64)
 CHUNK = 1024
 PIECES = 4
 

time: 36.1 us -> 36.1 us (level)
  no operation moved by 1% of the time
where the time goes in v9:
time: 36.1 us; the launch traced here: 35.9 us
  Pallas kernels  35.3 us (98%)
  between operations  0.64 us (2%)
    pallas_call x1, Pallas kernels, per_device(): pl.pallas_call(functools.partial(kernel, sections, n, q, pad), out_shape=...  34.2 us
    pallas_call x1, Pallas kernels, per_device(): pl.pallas_call(store_results, out_shape=shapes, in_specs=[anywhere, anywh...  1.11 us

profile of v9, /device:TPU:0, one launch (start us, length us, event | category | flops | bytes accessed | tf_op | source)
XLA Modules:
  0.0 35.9 jit_solution(7416984306411304105)
XLA Ops:
  0.6 34.2 %shard_map.68 = (bf16[1,128,5120]{2,1,0:T(8,128)(2,1)S(1)}, bf16[1,10240]{1,0:T(2,128)(2,1)S(1)}) custom-call(bf16[1,128,5120]{2,1,0:T(8,128)(2,1)} %x_hbm.1, bf16[1,128,5120]{2,1,0:T(8,128)(2,1)} %g_hbm.1, f32[1,5120]{1,0:T(1,128)} %gain_hbm.1, bf16[1,16,5120]{2,1,0:T(8,128)(2,1)} %down_hbm.1, bf16[1,16,5120]{2,1,0:T(8,128)(2,1)} %up_hbm.1), custom_call_target="tpu_custom_call" | custom-call | flops 125829120 | bytes 3932160 | tf_op jit(solution)/shard_map/pallas_call | solution.py:373
  34.8 1.1 %shard_map.69 = (bf16[1,128,5120]{2,1,0:T(8,128)(2,1)}, bf16[1,10240]{1,0:T(2,128)(2,1)}) custom-call(bf16[1,128,5120]{2,1,0:T(8,128)(2,1)S(1)} %get-tuple-element.4.passed_in, bf16[1,10240]{1,0:T(2,128)(2,1)S(1)} %get-tuple-element.5.pair_in), custom_call_target="tpu_custom_call" | custom-call | tf_op jit(solution)/shard_map/pallas_call | solution.py:417
